TPU v7x, 32 devices: a whole 2x2x4 slice. The times are simulated.
32 devices in a mesh: grp: 2 (over y), pts: 4 (over z), col: 2 (over x), sub: 2 (over core).
Axes of the slice: x: 2, y: 2, z: 4, core: 2. Of those that a mesh axis runs over, the one named last changes fastest.
Arguments:
- points: bfloat16 [32768, 256], P(('grp', 'pts', 'sub')), parts along dimension 0, may hold values from -12 to 12
- weights: bfloat16 [32768, 128], P(('grp', 'pts', 'sub')), parts along dimension 0, may hold values from -0.046875 to 0.046875
- tile_rows: int32 [4, 8, 128], P(('grp', 'col'), ('pts', 'sub')), parts along dimension 0, may hold values from 0 to 2047, as said below
- tile_count: int32 [4, 8], P(('grp', 'col')), parts along dimension 0, may hold values from 1 to 128, 512 in all within a row
- sketch_pick: int32 [4, 256], P(('grp', 'col')), parts along dimension 0, may hold values from 0 to 511, as said below
- block_targets: bfloat16 [4, 1024, 128], P(('grp', 'col'), ('pts', 'sub')), parts along dimension 0, may hold values from -4 to 4
- core_inv: float32 [1024, 512], P('grp'), parts along dimension 0, as said below
Outputs:
- block_grad: float32 [4, 1024, 128], P(('grp', 'col'), ('pts', 'sub')), parts along dimension 0
- direction: float32 [4, 1024, 128], P(('grp', 'col'), ('pts', 'sub')), parts along dimension 0
There are 2 independent parts, one for each index of `grp`. A program takes and returns all parts, laid end to end along the dimension named above; each array names one. Nothing has to cross between parts.
Inputs may be any that keep to these rules, and one draw needn't show every extreme that they name: For each owner o, the 256 entries tile_rows[:, o, :] are distinct; only slots below tile_count are used. `tile_count`: each row of 8 counts sums to 512, and its largest count is 128. `sketch_pick`: the entries of one row are distinct. `core_inv`: A full-rank matrix.
All inputs are finite; a program needn't handle non-finite values.
Results may differ from a plain program's by a relative error of at most 0.0003.
Values may be sent and summed in bfloat16 or wider, within the bound.
A program may use at most 64 MiB of HBM per device.

v0:
```python
import math

import jax
import jax.numpy as jnp
from jax import lax
from jax.sharding import PartitionSpec as P

RIDGE_COEF = 50.0
HIGHEST_PREC = lax.Precision.HIGHEST


def sq_norms(values):
    widened = values.astype(jnp.float32)
    return jnp.sum(widened * widened, axis=1)


def kernel_block(left_x, left_sq, right_x, right_sq):
    inner_prods = jnp.einsum("ik,jk->ij", left_x, right_x, preferred_element_type=jnp.float32)
    dist_sq = left_sq[:, None] + right_sq[None, :] - 2.0 * inner_prods
    return jnp.exp(-dist_sq / left_x.shape[1])


def pick_entry(table, position):
    return jnp.sum(jnp.where(jnp.arange(table.shape[0]) == position, table, 0))


def per_device(points, weights, tile_rows, tile_count, sketch_pick, block_targets, core_inv):
    slot_cap = tile_rows.shape[2]
    counts = tile_count[0]
    owner_total = counts.shape[0]
    live_total = owner_total * slot_cap // 2
    owner_idx = lax.axis_index(("pts", "sub"))
    offsets = jnp.cumsum(counts) - counts
    own_count = pick_entry(counts, owner_idx)
    slot_ids = jnp.arange(slot_cap, dtype=jnp.int32)
    used_float = (slot_ids < own_count).astype(jnp.float32)[:, None]
    own_rows = tile_rows[0, 0]
    own_x = jnp.where(used_float > 0, jnp.take(points, own_rows, axis=0), 0)
    own_alpha = jnp.take(weights, own_rows, axis=0).astype(jnp.float32)
    tile_x = lax.all_gather(own_x, ("pts", "sub"), axis=0, tiled=True)
    tile_sq = sq_norms(tile_x)
    slab_sq = sq_norms(points)
    slab_total = points.shape[0]
    slab_step = math.gcd(slab_total, 512)
    rank_ids = jnp.arange(live_total, dtype=jnp.int32)
    owner_of = jnp.sum((offsets[None, :] <= rank_ids[:, None]).astype(jnp.int32), axis=1) - 1
    owner_onehot = owner_of[:, None] == jnp.arange(owner_total)[None, :]
    live_slot = (
        owner_of * slot_cap
        + rank_ids
        - jnp.sum(jnp.where(owner_onehot, offsets[None, :], 0), axis=1)
    )

    def add_block(block_idx, running):
        slab_x = lax.dynamic_slice_in_dim(points, block_idx * slab_step, slab_step, 0)
        slab_w = lax.dynamic_slice_in_dim(weights, block_idx * slab_step, slab_step, 0).astype(
            jnp.float32
        )
        block_sq = lax.dynamic_slice_in_dim(slab_sq, block_idx * slab_step, slab_step, 0)
        kern_vals = kernel_block(tile_x, tile_sq, slab_x, block_sq)
        return running + jnp.dot(kern_vals, slab_w, precision=HIGHEST_PREC)

    start_sum = jnp.zeros((tile_x.shape[0], weights.shape[1]), jnp.float32)
    slab_part = lax.psum_scatter(
        lax.fori_loop(0, slab_total // slab_step, add_block, start_sum),
        ("pts", "sub"),
        scatter_dimension=0,
        tiled=True,
    )
    targets = block_targets[0].astype(jnp.float32)
    block_grad = used_float * (slab_part + RIDGE_COEF * own_alpha - targets)
    sketch_slot = jnp.take(live_slot, sketch_pick[0], axis=0)
    sketch_local = jnp.take(tile_x, sketch_slot, axis=0)
    sketch_x = lax.all_gather(sketch_local, "col", axis=0, tiled=True)
    sketch_kern = used_float * kernel_block(own_x, sq_norms(own_x), sketch_x, sq_norms(sketch_x))
    local_proj = jnp.dot(sketch_kern.T, block_grad, precision=HIGHEST_PREC)
    projected = lax.psum(local_proj, ("pts", "col", "sub"))
    weighted = jnp.dot(core_inv, projected, precision=HIGHEST_PREC)
    direction = used_float * (block_grad - jnp.dot(sketch_kern, weighted, precision=HIGHEST_PREC))
    return (block_grad[None], direction[None])


def solution(mesh):
    in_specs = (
        P(("grp", "pts", "sub"), None),
        P(("grp", "pts", "sub"), None),
        P(("grp", "col"), ("pts", "sub"), None),
        P(("grp", "col"), None),
        P(("grp", "col"), None),
        P(("grp", "col"), ("pts", "sub"), None),
        P("grp", None),
    )
    out_specs = (P(("grp", "col"), ("pts", "sub"), None), P(("grp", "col"), ("pts", "sub"), None))
    return jax.shard_map(
        per_device, mesh=mesh, in_specs=in_specs, out_specs=out_specs, check_vma=False
    )
```

profile of v0, /device:TPU:1, one launch (start us, length us, event | category | flops | bytes accessed | tf_op | source)
XLA Modules:
  0.0 187.1 jit_solution(5780408351962476899)
XLA Ops:
  8.0 1.6 multiply_reduce_fusion
  9.6 2.1 %gather_fusion = bf16[128,256]{1,0:T(8,128)(2,1)S(1)} fusion(bf16[2048,256]{1,0:T(8,128)(2,1)} %param.9, s32[1024]{0:T(1024)S(1)} %pad_clamp_fusion.2), kind=kCustom, calls=%fused_computation | custom fusion | bytes 131584 | tf_op jit(solution)/shard_map/jit(_take)/gather | solution.py:38
  11.7 1.3 fusion.29
  13.0 1.3 compare_and_fusion.1
  14.5 16.5 %all_gather.6 = bf16[1024,256]{1,0:T(8,128)(2,1)S(1)} all-gather(bf16[128,256]{1,0:T(8,128)(2,1)S(1)} %get-tuple-element.166), channel_id=1, replica_groups=mesh['grp'=2,'pts'=4,'col'=2,'sub'=2] {'pts','sub'}, dimensions={0}, use_global_device_ids=true | all-gather | bytes 589824 | tf_op jit(solution)/shard_map/all_gather | solution.py:40
  31.7 22.2 %while.14 = (s32[]{:T(128)}, f32[1024,128]{1,0:T(8,128)}, f32[1024]{0:T(1024)S(1)}, f32[2048]{0:T(1024)S(1)}, bf16[2048,256]{1,0:T(8,128)(2,1)}, /*index=5*/bf16...) while((s32[]{:T(128)}, f32[1024,128]{1,0:T(8,128)}, ...), condition=%wide.region_4.5_spmd.clone, body=%wide.region_3.4_spmd.clone.sunk | while | flops 1076625408 | bytes 6170809 | solution.py:65
  31.7 1.6 fusion.52
  33.4 3.7 %fusion.53 = f32[1024,128]{1,0:T(8,128)} fusion(f32[512,1024]{1,0:T(8,128)S(1)} %fusion.52, f32[512]{0:T(512)S(1)} %dynamic_slice.33, f32[1024]{0:T(1024)S(1)} %get-tuple-element.236, f32[1024,128]{1,0:T(8,128)} %get-tuple-element.224, pred[]{:T(512)S(6)} %compare.3, bf16[2048,128]{1,0:T(8,128)(2,1)} %get-tuple-element.240, s32[]{:T(128)S(6)} %select_n.155), kind=kOutput, calls=%fused_computation.11.clone.1 | convolution fusion | flops 808189952 | bytes 3282949 | tf_op jit(solution)/shard_map/while/body/eval_jaxpr/dot_general | solution.py:61
  37.2 1.6 fusion.52
  38.8 3.9 %fusion.53 = f32[1024,128]{1,0:T(8,128)} fusion(f32[512,1024]{1,0:T(8,128)S(1)} %fusion.52, f32[512]{0:T(512)S(1)} %dynamic_slice.33, f32[1024]{0:T(1024)S(1)} %get-tuple-element.236, f32[1024,128]{1,0:T(8,128)} %get-tuple-element.224, pred[]{:T(512)S(6)} %compare.3, bf16[2048,128]{1,0:T(8,128)(2,1)} %get-tuple-element.240, s32[]{:T(128)S(6)} %select_n.155), kind=kOutput, calls=%fused_computation.11.clone.1 | convolution fusion | flops 808189952 | bytes 3282949 | tf_op jit(solution)/shard_map/while/body/eval_jaxpr/dot_general | solution.py:61
  42.8 1.6 fusion.52
  44.4 3.9 %fusion.53 = f32[1024,128]{1,0:T(8,128)} fusion(f32[512,1024]{1,0:T(8,128)S(1)} %fusion.52, f32[512]{0:T(512)S(1)} %dynamic_slice.33, f32[1024]{0:T(1024)S(1)} %get-tuple-element.236, f32[1024,128]{1,0:T(8,128)} %get-tuple-element.224, pred[]{:T(512)S(6)} %compare.3, bf16[2048,128]{1,0:T(8,128)(2,1)} %get-tuple-element.240, s32[]{:T(128)S(6)} %select_n.155), kind=kOutput, calls=%fused_computation.11.clone.1 | convolution fusion | flops 808189952 | bytes 3282949 | tf_op jit(solution)/shard_map/while/body/eval_jaxpr/dot_general | solution.py:61
  48.4 1.6 fusion.52
  50.0 3.9 %fusion.53 = f32[1024,128]{1,0:T(8,128)} fusion(f32[512,1024]{1,0:T(8,128)S(1)} %fusion.52, f32[512]{0:T(512)S(1)} %dynamic_slice.33, f32[1024]{0:T(1024)S(1)} %get-tuple-element.236, f32[1024,128]{1,0:T(8,128)} %get-tuple-element.224, pred[]{:T(512)S(6)} %compare.3, bf16[2048,128]{1,0:T(8,128)(2,1)} %get-tuple-element.240, s32[]{:T(128)S(6)} %select_n.155), kind=kOutput, calls=%fused_computation.11.clone.1 | convolution fusion | flops 808189952 | bytes 3282949 | tf_op jit(solution)/shard_map/while/body/eval_jaxpr/dot_general | solution.py:61
  54.5 1.9 %gather_fusion.2 = s32[256]{0:T(256)S(1)} fusion(s32[512]{0:T(512)S(1)} %add_subtract_fusion, s32[1024]{0:T(1024)S(1)} %pad_clamp_fusion.1), kind=kCustom, calls=%fused_computation.2 | custom fusion | bytes 3072 | tf_op jit(solution)/shard_map/jit(_take)/gather | solution.py:72
  56.5 1.8 gather_fusion.1
  58.2 1.2 gather_fusion.3
  59.5 5.7 %all_gather.7 = bf16[512,256]{1,0:T(8,128)(2,1)S(1)} all-gather(bf16[256,256]{1,0:T(8,128)(2,1)S(1)} %broadcast_select_fusion), channel_id=1, replica_groups=mesh['grp'=2,'pts'=4,'col'=2,'sub'=2] {'col'}, dimensions={0}, use_global_device_ids=true | all-gather | bytes 393216 | tf_op jit(solution)/shard_map/all_gather | solution.py:74
  66.3 15.9 %reduce-scatter.2.cloned.1.call-done = f32[128,128]{1,0:T(8,128)} async-done(((f32[1024,128]{1,0:T(8,128)}), f32[128,128]{1,0:T(8,128)}) %reduce-scatter.2.cloned.1.call-update) | async-done | bytes 65552 | tf_op jit(solution)/shard_map/reduce_scatter | solution.py:64
  82.2 0.9 fusion.28
  83.2 1.3 fusion.31
  84.5 92.5 %all-reduce.2.cloned.1.call-done = f32[512,128]{1,0:T(8,128)} async-done(((f32[512,128]{1,0:T(8,128)}), f32[512,128]{1,0:T(8,128)}) %all-reduce.2.cloned.1.call-update) | async-done | bytes 262160 | tf_op jit(solution)/shard_map/psum | solution.py:77
  177.0 2.2 %fusion.32 = f32[128,512]{1,0:T(8,128)S(1)} fusion(f32[512,128]{1,0:T(8,128)} %all-reduce.2.cloned.1.call-done, f32[512,512]{1,0:T(8,128)S(1)} %copy-done), kind=kOutput, calls=%fused_computation.66 | convolution fusion | flops 402653184 | bytes 1572864 | tf_op jit(solution)/shard_map/dot_general | solution.py:78
  179.2 1.0 fusion.27
  (42 shorter events, 3.7 us)
Async XLA Ops:
  7.2 169.8 %copy-start = (f32[512,512]{1,0:T(8,128)S(1)}, f32[512,512]{1,0:T(8,128)}, u32[]{:S(2)}) copy-start(f32[512,512]{1,0:T(8,128)} %param.15) | copy-start | bytes 3145732
  7.2 75.0 %reduce-scatter.2.cloned.1.call-start = ((), (), s32[]{:S(2)}) async-start(), calls=%async_computation.1 | async-start | bytes 589824 | tf_op jit(solution)/shard_map/reduce_scatter | solution.py:64
  30.9 0.8 copy-start.1
  31.7 22.3 %copy-start.6 = (s32[1,8]{1,0:T(1,128)S(1)}, s32[1,8]{1,0:T(1,128)}, u32[]{:S(2)}) copy-start(s32[1,8]{1,0:T(1,128)} %param.12) | copy-start | bytes 100
  31.7 22.7 %copy-start.5 = (s32[1,256]{1,0:T(1,128)S(1)}, s32[1,256]{1,0:T(1,128)}, u32[]{:S(2)}) copy-start(s32[1,256]{1,0:T(1,128)} %param.13) | copy-start | bytes 3076
  54.0 4.2 %copy-start.2 = (bf16[1024,256]{1,0:T(8,128)(2,1)S(1)}, bf16[1024,256]{1,0:T(8,128)(2,1)}, u32[]{:S(2)}) copy-start(bf16[1024,256]{1,0:T(8,128)(2,1)} %get-tuple-element.247) | copy-start | bytes 1572868
  54.0 123.0 %all-reduce.2.cloned.1.call-start = ((), (), s32[]{:S(2)}) async-start(), calls=%async_computation.2 | async-start | bytes 524288 | tf_op jit(solution)/shard_map/psum | solution.py:77
  54.3 28.0 %copy-start.4 = (bf16[1,128,128]{2,1,0:T(8,128)(2,1)S(1)}, bf16[1,128,128]{2,1,0:T(8,128)(2,1)}, u32[]{:S(2)}) copy-start(bf16[1,128,128]{2,1,0:T(8,128)(2,1)} %param.14) | copy-start | bytes 98308
  83.2 97.1 %copy-start.3 = (f32[128,128]{1,0:T(8,128)}, f32[128,128]{1,0:T(8,128)S(1)}, u32[]{:S(2)}) copy-start(f32[128,128]{1,0:T(8,128)S(1)} %fusion.28) | copy-start | bytes 196612
Sparse Core Ops, SparseCore 0:
  54.1 28.0 reduce-scatter.1
  86.0 90.9 all-reduce.1
where the time goes:
time: 188 us; the launch traced here: 187 us
  waiting for transfers between devices  108 us (57%)
  matrix products  26.7 us (14%)
  blocking collectives  22.2 us (12%)
  between operations  14.2 us (8%)
  local copies, waits for them, and re-layouts  7.9 us (4%)
  other arithmetic  7.55 us (4%)
    psum x1, waiting for transfers between devices, per_device(): projected = lax.psum(local_proj, ('pts', 'col', 'sub'))  92.5 us
    all_gather x1, blocking collectives, per_device(): tile_x = lax.all_gather(own_x, ('pts', 'sub'), axis=0, tiled=True)  16.5 us
    reduce_scatter x1, waiting for transfers between devices, per_device(): lax.psum_scatter(lax.fori_loop(0, slab_total // slab_step, add_block, sta...  15.9 us
    dot_general x4, matrix products, add_block(): return running + jnp.dot(kern_vals, slab_w, precision=HIGHEST_PREC)  15.5 us
    dot_general x5, matrix products, kernel_block(): jnp.einsum('ik,jk->ij', left_x, right_x, preferred_element_type=jnp.float32)  6.63 us
    all_gather x1, blocking collectives, per_device(): sketch_x = lax.all_gather(sketch_local, 'col', axis=0, tiled=True)  5.7 us
  transfers between devices with their start and end apart: 2, of which 2 were waited for; matrix products, arithmetic and copies ran while one was open for 3% of the time, Pallas kernels for 0%

commit v1 on v0

v1 whole, which is shorter than its diff:
```python
import functools
import math

import jax
import jax.numpy as jnp
from jax import lax
from jax.experimental import pallas as pl
from jax.experimental.pallas import tpu as pltpu
from jax.sharding import PartitionSpec as P

RIDGE_COEF = 50.0
MESH = pl.DeviceIdType.MESH
F32 = jnp.float32
BF16 = jnp.bfloat16
NN = (((1,), (0,)), ((), ()))
NT = (((1,), (1,)), ((), ()))


def mm(left, right, dims=NN):
    return lax.dot_general(left, right, dims, preferred_element_type=F32)


def split2(value):
    high = value.astype(BF16)
    return high, (value - high.astype(F32)).astype(BF16)


def mm3(left, right, dims=NN):
    (lh, ll), (rh, rl) = left, right
    return mm(lh, rh, dims) + (mm(lh, rl, dims) + mm(ll, rh, dims))


def mix(index, step, total):
    if total & (total - 1):
        return (index + step) % total
    out, bit = 0, 1
    while bit < total:
        out = out + bit * (((index // bit) % 2 + (step // bit) % 2) % 2)
        bit *= 2
    return out


def each(low, high, body):
    if high - low <= 8:
        for i in range(low, high):
            body(i)
    elif high > low:
        lax.fori_loop(low, high, lambda i, c: (body(i), c)[1], 0)


def sq_col(x):
    wide = x.astype(F32)
    return jnp.sum(wide * wide, axis=1, keepdims=True)


def sq_row(x):
    wide = x.astype(F32)
    high, low = split2(wide * wide)
    ones = jnp.ones((8, x.shape[1]), BF16)
    return (mm(ones, high, NT) + mm(ones, low, NT))[0:1, :]


def column(row):
    return jnp.transpose(jnp.broadcast_to(row, (8, row.shape[1])))[:, 0:1]


def body(
    sizes, cnt_ref, rows_ref, pick_ref, targ_ref, points_hbm, weights_hbm, core_hbm,
    bg_ref, dir_ref,
    pts_v, wts_v, core_v, psq, core_hi, core_lo,
    xbuf, part, subr, lsum, lrec, skx, kern, pj, pjr, psum, prec, fbuf,
    in_sem, ag_s, ag_r, fw_s, fw_r, sb_s, sb_r, ln_s, ln_r, sk_s, sk_r,
    pe_s, pe_r, rs_s, rs_r, fa_s, fa_r, ff_s, ff_r,
):
    n_p, n_c, n_s, cap, width, outs, n_pts, n_sk, rank, piece = sizes
    n_q = n_p * n_c
    half = rank // n_s
    owners = n_p * n_s
    p = lax.axis_index("pts")
    c = lax.axis_index("col")
    s = lax.axis_index("sub")
    q = p * n_c + c
    other = 1 - s
    sibling = {"sub": other}
    c2 = math.log2(math.e) / width

    def at_q(k):
        peer = mix(q, k, n_q)
        return peer, {"pts": peer // n_c, "col": peer % n_c}

    def rc(src, dst, ssem, rsem, dev):
        return pltpu.make_async_remote_copy(
            src_ref=src, dst_ref=dst, send_sem=ssem, recv_sem=rsem,
            device_id=dev, device_id_type=MESH,
        )

    in_pts = pltpu.make_async_copy(points_hbm, pts_v, in_sem.at[0])
    in_wts = pltpu.make_async_copy(weights_hbm, wts_v, in_sem.at[1])
    in_core = pltpu.make_async_copy(core_hbm, core_v, in_sem.at[2])
    in_pts.start()
    in_wts.start()
    in_core.start()

    barrier = pltpu.get_barrier_semaphore()
    pl.semaphore_signal(barrier, inc=1, device_id=sibling, device_id_type=MESH)

    def greet(k):
        pl.semaphore_signal(barrier, inc=1, device_id=at_q(k)[1], device_id_type=MESH)

    each(1, n_q, greet)

    own_count = cnt_ref[0, p * n_s + s]
    used = lax.broadcasted_iota(jnp.int32, (cap, 1), 0) < own_count
    rows = jnp.where(used, column(rows_ref[0].astype(F32)), -1.0)
    ids = lax.broadcasted_iota(jnp.int32, (1, n_pts), 1).astype(F32)
    pick_rows = jnp.where(rows == ids, 1.0, 0.0).astype(BF16)
    in_pts.wait()
    xbuf[p, s] = mm(pick_rows, pts_v[...]).astype(BF16)
    pl.semaphore_wait(barrier, n_q)

    def fw(pk, slot):
        return rc(xbuf.at[pk, slot], xbuf.at[pk, slot], fw_s.at[pk], fw_r.at[pk], sibling)

    fw(p, s).start()

    def ag_send(k):
        peer = mix(p, k, n_p)
        rc(xbuf.at[p, s], xbuf.at[p, s], ag_s.at[peer], ag_r.at[p], {"pts": peer}).start()

    each(1, n_p, ag_send)

    in_wts.wait()
    alpha = mm(pick_rows, wts_v[...])
    psq[...] = sq_row(pts_v[...]) * c2

    def lane_forward(k):
        pk = mix(p, k, n_p)
        rc(xbuf.at[pk, s], xbuf.at[pk, s], ag_s.at[pk], ag_r.at[pk], {"pts": pk}).wait_recv()
        fw(pk, s).start()

    step = math.gcd(n_pts, 512)

    def compute(k):
        pk = mix(p, k, n_p)
        fw(pk, other).wait_recv()
        x = xbuf[pk].reshape(n_s * cap, width)
        left = sq_col(x) * c2

        def add(i, acc):
            at = pl.ds(pl.multiple_of(i * step, step), step)
            inner = mm(x, pts_v[at, :], NT)
            vals = jnp.exp2((inner * (2.0 * c2) - left) - psq[:, at])
            high, low = split2(vals)
            w = wts_v[at, :]
            return acc + (mm(high, w) + mm(low, w))

        acc = lax.fori_loop(0, n_pts // step, add, jnp.zeros((n_s * cap, outs), F32))
        part[pk] = acc.reshape(n_s, cap, outs)
        rc(part.at[pk, other], subr.at[pk], sb_s.at[pk], sb_r.at[pk], sibling).start()

    def sub_wait(pk):
        rc(part.at[pk, other], subr.at[pk], sb_s.at[pk], sb_r.at[pk], sibling).wait_recv()

    def lane_send(k):
        pk = mix(p, k, n_p)
        sub_wait(pk)
        lsum[pk] = part[pk, s] + subr[pk]
        rc(lsum.at[pk], lrec.at[p], ln_s.at[pk], ln_r.at[p], {"pts": pk}).start()

    compute(0)
    if n_p > 1:
        lane_forward(1)

        def stage(k):
            lane_forward(k + 1)
            compute(k)

            @pl.when(k >= 2)
            def _():
                lane_send(k - 1)

        if n_p <= 4:
            for k in range(1, n_p - 1):
                lane_forward(k + 1)
                compute(k)
                if k >= 2:
                    lane_send(k - 1)
        else:
            lax.fori_loop(1, n_p - 1, lambda k, z: (stage(k), z)[1], 0)
        compute(n_p - 1)
        if n_p > 2:
            lane_send(n_p - 2)

    slot = lax.broadcasted_iota(jnp.int32, (1, owners * cap), 1)
    rank_of = jnp.full((1, owners * cap), -1, jnp.int32)
    before = 0
    for o in range(owners):
        have = cnt_ref[0, o]
        local = slot - o * cap
        rank_of = jnp.where((local >= 0) & (local < have), local + before, rank_of)
        before = before + have
    picks = column(pick_ref[...].astype(F32))
    onehot = jnp.where(picks == rank_of.astype(F32), 1.0, 0.0).astype(BF16)
    skx[c] = mm(onehot, xbuf[...].reshape(owners * cap, width)).astype(BF16)

    def sk(ck, mine):
        return rc(skx.at[mine], skx.at[mine], sk_s.at[ck], sk_r.at[mine], {"col": ck})

    each(1, n_c, lambda k: sk(mix(c, k, n_c), c).start())
    if n_p > 1:
        lane_send(n_p - 1)

    in_core.wait()
    high, low = split2(core_v[...])
    core_hi[...] = high
    core_lo[...] = low

    each(1, n_c, lambda k: sk(mix(c, k, n_c), mix(c, k, n_c)).wait_recv())
    own_x = xbuf[p, s]
    sketch = skx[...].reshape(rank, width)
    kern_t = jnp.exp2((mm(sketch, own_x, NT) * (2.0 * c2) - sq_col(sketch) * c2) - sq_row(own_x) * c2)
    kern_t = split2(kern_t)
    kern[...] = jnp.exp2((mm(own_x, sketch, NT) * (2.0 * c2) - sq_col(own_x) * c2) - sq_row(sketch) * c2)

    sub_wait(p)
    slab = part[p, s] + subr[p]
    for k in range(1, n_p):
        pk = mix(p, k, n_p)
        rc(lsum.at[pk], lrec.at[pk], ln_s.at[pk], ln_r.at[pk], {"pts": pk}).wait_recv()
        slab = slab + lrec[pk]
    used_f = used.astype(F32)
    grad = used_f * (slab + RIDGE_COEF * alpha - targ_ref[0].astype(F32))
    bg_ref[0] = grad

    proj = mm3(kern_t, split2(grad))
    if half < n_q * piece:
        pj[...] = jnp.zeros_like(pj)
    for h in range(n_s):
        pj[h, 0:half, :] = proj[h * half:(h + 1) * half, :]
    pe = rc(pj.at[other], pjr, pe_s, pe_r, sibling)
    pe.start()
    pe.wait_recv()
    psum[...] = (pj[s] + pjr[...]).reshape(n_q, piece, outs)

    def rs(k, mine):
        peer, dev = at_q(k)
        return rc(psum.at[peer], prec.at[mine(peer)], rs_s.at[peer], rs_r.at[mine(peer)], dev)

    each(1, n_q, lambda k: rs(k, lambda peer: q).start())
    total = psum[q]
    if n_q <= 8:
        for k in range(1, n_q):
            rs(k, lambda peer: peer).wait_recv()
            total = total + prec[mix(q, k, n_q)]
    else:
        def gain(k, run):
            rs(k, lambda peer: peer).wait_recv()
            return run + prec[mix(q, k, n_q)]

        total = lax.fori_loop(1, n_q, gain, total)
    fbuf[s, q] = total

    def fa(k, mine):
        peer, dev = at_q(k)
        at = fbuf.at[s, mine(peer)]
        return rc(at, at, fa_s.at[peer], fa_r.at[mine(peer)], dev)

    def ff(peer, side):
        at = fbuf.at[side, peer]
        return rc(at, at, ff_s.at[peer], ff_r.at[peer], sibling)

    each(1, n_q, lambda k: fa(k, lambda peer: q).start())
    ff(q, s).start()

    def relay(k):
        fa(k, lambda peer: peer).wait_recv()
        ff(mix(q, k, n_q), s).start()

    each(1, n_q, relay)
    each(0, n_q, lambda k: ff(mix(q, k, n_q), other).wait_recv())

    weighted = jnp.zeros((rank, outs), F32)
    for h in range(n_s):
        block = fbuf[h].reshape(n_q * piece, outs)[0:half, :]
        cols = slice(h * half, (h + 1) * half)
        weighted = weighted + mm3((core_hi[:, cols], core_lo[:, cols]), split2(block))
    dir_ref[0] = used_f * (grad - mm3(split2(kern[...]), split2(weighted)))

    def lane_done(k):
        pk = mix(p, k, n_p)
        rc(xbuf.at[p, s], xbuf.at[p, s], ag_s.at[pk], ag_r.at[p], {"pts": pk}).wait_send()
        rc(lsum.at[pk], lrec.at[p], ln_s.at[pk], ln_r.at[p], {"pts": pk}).wait_send()

    def chip_done(k):
        pk = mix(p, k, n_p)
        fw(pk, s).wait_send()
        rc(part.at[pk, other], subr.at[pk], sb_s.at[pk], sb_r.at[pk], sibling).wait_send()

    def piece_done(k):
        rs(k, lambda peer: q).wait_send()
        fa(k, lambda peer: q).wait_send()

    each(1, n_p, lane_done)
    each(0, n_p, chip_done)
    each(1, n_c, lambda k: sk(mix(c, k, n_c), c).wait_send())
    pe.wait_send()
    each(1, n_q, piece_done)
    each(0, n_q, lambda k: ff(mix(q, k, n_q), s).wait_send())


def per_device(mesh_sizes, points, weights, tile_rows, tile_count, sketch_pick, block_targets, core_inv):
    n_p, n_c, n_s = mesh_sizes
    cap = tile_rows.shape[2]
    n_pts, width = points.shape
    outs = weights.shape[1]
    n_sk = sketch_pick.shape[1]
    rank = core_inv.shape[0]
    n_q = n_p * n_c
    piece = max(8, -(-rank // (n_s * n_q)))
    sizes = (n_p, n_c, n_s, cap, width, outs, n_pts, n_sk, rank, piece)
    vmem = pl.BlockSpec(memory_space=pltpu.VMEM)
    smem = pl.BlockSpec(memory_space=pltpu.SMEM)
    hbm = pl.BlockSpec(memory_space=pl.ANY)
    dma = pltpu.SemaphoreType.DMA
    out = jax.ShapeDtypeStruct((1, cap, outs), F32)
    return pl.pallas_call(
        functools.partial(body, sizes),
        out_shape=(out, out),
        in_specs=[smem, vmem, vmem, vmem, hbm, hbm, hbm],
        out_specs=(vmem, vmem),
        scratch_shapes=[
            pltpu.VMEM((n_pts, width), BF16),
            pltpu.VMEM((n_pts, outs), BF16),
            pltpu.VMEM((rank, rank), F32),
            pltpu.VMEM((1, n_pts), F32),
            pltpu.VMEM((rank, rank), BF16),
            pltpu.VMEM((rank, rank), BF16),
            pltpu.VMEM((n_p, n_s, cap, width), BF16),
            pltpu.VMEM((n_p, n_s, cap, outs), F32),
            pltpu.VMEM((n_p, cap, outs), F32),
            pltpu.VMEM((n_p, cap, outs), F32),
            pltpu.VMEM((n_p, cap, outs), F32),
            pltpu.VMEM((n_c, n_sk, width), BF16),
            pltpu.VMEM((cap, rank), F32),
            pltpu.VMEM((n_s, n_q * piece, outs), F32),
            pltpu.VMEM((n_q * piece, outs), F32),
            pltpu.VMEM((n_q, piece, outs), F32),
            pltpu.VMEM((n_q, piece, outs), F32),
            pltpu.VMEM((n_s, n_q, piece, outs), F32),
            dma((3,)),
            dma((n_p,)), dma((n_p,)),
            dma((n_p,)), dma((n_p,)),
            dma((n_p,)), dma((n_p,)),
            dma((n_p,)), dma((n_p,)),
            dma((n_c,)), dma((n_c,)),
            dma(()), dma(()),
            dma((n_q,)), dma((n_q,)),
            dma((n_q,)), dma((n_q,)),
            dma((n_q,)), dma((n_q,)),
        ],
        compiler_params=pltpu.CompilerParams(
            collective_id=0, has_side_effects=True, vmem_limit_bytes=48 * 1024 * 1024
        ),
    )(tile_count, tile_rows, sketch_pick, block_targets, points, weights, core_inv)


def solution(mesh):
    in_specs = (
        P(("grp", "pts", "sub"), None),
        P(("grp", "pts", "sub"), None),
        P(("grp", "col"), ("pts", "sub"), None),
        P(("grp", "col"), None),
        P(("grp", "col"), None),
        P(("grp", "col"), ("pts", "sub"), None),
        P("grp", None),
    )
    out_specs = (P(("grp", "col"), ("pts", "sub"), None), P(("grp", "col"), ("pts", "sub"), None))
    mesh_sizes = (mesh.shape["pts"], mesh.shape["col"], mesh.shape["sub"])
    return jax.shard_map(
        functools.partial(per_device, mesh_sizes), mesh=mesh, in_specs=in_specs,
        out_specs=out_specs, check_vma=False,
    )
```

time: 188 us -> 48.6 us (0.26)
  waiting for transfers between devices: 108 us -> 0 us
  Pallas kernels: 0 us -> 40.1 us
  matrix products: 26.7 us -> 0 us
  blocking collectives: 22.2 us -> 0 us
  between operations: 14.2 us -> 0.66 us
  other arithmetic: 7.55 us -> 0 us
    psum x1 -> x0, waiting for transfers between devices: 92.5 us -> none  [per_device(): projected = lax.psum(local_proj, ('pts', 'col', 'sub'))]
    pallas_call x0 -> x1, Pallas kernels: none -> 40.1 us  [per_device(): pl.pallas_call(functools.partial(body, sizes), out_shape=(out, out), in_s...]
    dot_general x12 -> x0, matrix products: 26.7 us -> none  [the longest x4 15.5 us: add_block(): return running + jnp.dot(kern_vals, slab_w, precision=HIGHEST_PREC)]
    all_gather x2 -> x0, blocking collectives: 22.2 us -> none  [the longest x1 16.5 us: per_device(): tile_x = lax.all_gather(own_x, ('pts', 'sub'), axis=0, tiled=True)]
    reduce_scatter x1 -> x0, waiting for transfers between devices: 15.9 us -> none  [per_device(): lax.psum_scatter(lax.fori_loop(0, slab_total // slab_step, add_block, sta...]
    gather x4 -> x0, local copies, waits for them, and re-layouts: 6.98 us -> none  [the longest x1 2.12 us: per_device(): own_x = jnp.where(used_float > 0, jnp.take(points, own_rows, axis=0), 0)]
    unnamed x14 -> x16, local copies, waits for them, and re-layouts: 0.6 us -> 7.49 us
    reduce_sum x7 -> x0, other arithmetic: 3.58 us -> none  [the longest x4 2.11 us: sq_norms(): return jnp.sum(widened * widened, axis=1)]
  transfers between devices with their start and end apart: 2 -> 0, of which waited for: 2 -> 0; matrix products, arithmetic and copies ran while one was open for 3% -> 0% of each run, Pallas kernels for 0% -> 0%
where the time goes in v1:
time: 48.6 us; the launch traced here: 48.3 us
  Pallas kernels  40.1 us (83%)
  local copies, waits for them, and re-layouts  7.49 us (15%)
  between operations  0.66 us (1%)
    pallas_call x1, Pallas kernels, per_device(): pl.pallas_call(functools.partial(body, sizes), out_shape=(out, out), in_s...  40.1 us
    unnamed x16, local copies, waits for them, and re-layouts  7.49 us

profile of v1, /device:TPU:1, one launch (start us, length us, event | category | flops | bytes accessed | tf_op | source)
XLA Modules:
  0.0 48.3 jit_solution(4926257211401963503)
XLA Ops:
  0.6 0.0 copy-start
  0.6 1.2 %copy-done = bf16[2048,256]{1,0:T(8,128)(2,1)S(1)} copy-done((bf16[2048,256]{1,0:T(8,128)(2,1)S(1)}, bf16[2048,256]{1,0:T(8,128)(2,1)}, u32[]{:S(2)}) %copy-start) | copy-done | bytes 1048600
  1.9 0.0 copy-start.1
  1.9 1.2 %copy-done.1 = f32[512,512]{1,0:T(8,128)S(1)} copy-done((f32[512,512]{1,0:T(8,128)S(1)}, f32[512,512]{1,0:T(8,128)}, u32[]{:S(2)}) %copy-start.1) | copy-done | bytes 1048600
  3.1 0.0 copy-start.2
  3.1 1.0 %copy-done.2 = bf16[2048,128]{1,0:T(8,128)(2,1)S(1)} copy-done((bf16[2048,128]{1,0:T(8,128)(2,1)S(1)}, bf16[2048,128]{1,0:T(8,128)(2,1)}, u32[]{:S(2)}) %copy-start.2) | copy-done | bytes 524312
  4.1 0.0 copy-start.3
  4.1 0.8 %copy-done.3 = bf16[1,128,128]{2,1,0:T(8,128)(2,1)S(1)} copy-done((bf16[1,128,128]{2,1,0:T(8,128)(2,1)S(1)}, bf16[1,128,128]{2,1,0:T(8,128)(2,1)}, u32[]{:S(2)}) %copy-start.3) | copy-done | bytes 32792
  4.9 0.0 copy-start.4
  4.9 0.7 %copy-done.4 = s32[1,256]{1,0:T(1,128)S(1)} copy-done((s32[1,256]{1,0:T(1,128)S(1)}, s32[1,256]{1,0:T(1,128)}, u32[]{:S(2)}) %copy-start.4) | copy-done | bytes 1048
  5.6 0.0 copy-start.5
  5.6 0.7 %copy-done.5 = s32[1,8]{1,0:T(1,128)S(1)} copy-done((s32[1,8]{1,0:T(1,128)S(1)}, s32[1,8]{1,0:T(1,128)}, u32[]{:S(2)}) %copy-start.5) | copy-done | bytes 56
  6.2 0.0 copy-start.6
  6.2 0.7 %copy-done.6 = s32[1,1,128]{2,1,0:T(1,128)S(1)} copy-done((s32[1,1,128]{2,1,0:T(1,128)S(1)}, s32[1,1,128]{2,1,0:T(1,128)}, u32[]{:S(2)}) %copy-start.6) | copy-done | bytes 536
  6.9 40.1 %shard_map.86 = (f32[1,128,128]{2,1,0:T(8,128)S(1)}, f32[1,128,128]{2,1,0:T(8,128)S(1)}) custom-call(s32[1,8]{1,0:T(1,128)S(1)} %copy-done.5, s32[1,1,128]{2,1,0:T(1,128)S(1)} %copy-done.6, s32[1,256]{1,0:T(1,128)S(1)} %copy-done.4, bf16[1,128,128]{2,1,0:T(8,128)(2,1)S(1)} %copy-done.3, bf16[2048,256]{1,0:T(8,128)(2,1)S(1)} %copy-done, ...), custom_call_target="tpu_custom_call" | custom-call | tf_op jit(solution)/shard_map/pallas_call | solution.py:326
  47.0 0.6 %copy.11 = f32[1,128,128]{2,1,0:T(8,128)} copy(f32[1,128,128]{2,1,0:T(8,128)S(1)} %get-tuple-element.4) | data formatting | bytes 131072
  47.7 0.6 %copy.12 = f32[1,128,128]{2,1,0:T(8,128)} copy(f32[1,128,128]{2,1,0:T(8,128)S(1)} %get-tuple-element.5) | data formatting | bytes 131072
Async XLA Ops:
  0.6 1.2 %copy-start = (bf16[2048,256]{1,0:T(8,128)(2,1)S(1)}, bf16[2048,256]{1,0:T(8,128)(2,1)}, u32[]{:S(2)}) copy-start(bf16[2048,256]{1,0:T(8,128)(2,1)} %points_hbm.1) | copy-start | bytes 3145732
  1.9 1.2 %copy-start.1 = (f32[512,512]{1,0:T(8,128)S(1)}, f32[512,512]{1,0:T(8,128)}, u32[]{:S(2)}) copy-start(f32[512,512]{1,0:T(8,128)} %core_hbm.1) | copy-start | bytes 3145732
  3.1 1.0 %copy-start.2 = (bf16[2048,128]{1,0:T(8,128)(2,1)S(1)}, bf16[2048,128]{1,0:T(8,128)(2,1)}, u32[]{:S(2)}) copy-start(bf16[2048,128]{1,0:T(8,128)(2,1)} %weights_hbm.1) | copy-start | bytes 1572868
  4.1 0.8 %copy-start.3 = (bf16[1,128,128]{2,1,0:T(8,128)(2,1)S(1)}, bf16[1,128,128]{2,1,0:T(8,128)(2,1)}, u32[]{:S(2)}) copy-start(bf16[1,128,128]{2,1,0:T(8,128)(2,1)} %targ_ref.1) | copy-start | bytes 98308
  4.9 0.7 %copy-start.4 = (s32[1,256]{1,0:T(1,128)S(1)}, s32[1,256]{1,0:T(1,128)}, u32[]{:S(2)}) copy-start(s32[1,256]{1,0:T(1,128)} %pick_ref.1) | copy-start | bytes 3076
  5.6 0.7 %copy-start.5 = (s32[1,8]{1,0:T(1,128)S(1)}, s32[1,8]{1,0:T(1,128)}, u32[]{:S(2)}) copy-start(s32[1,8]{1,0:T(1,128)} %cnt_ref.1) | copy-start | bytes 100
  6.2 0.7 %copy-start.6 = (s32[1,1,128]{2,1,0:T(1,128)S(1)}, s32[1,1,128]{2,1,0:T(1,128)}, u32[]{:S(2)}) copy-start(s32[1,1,128]{2,1,0:T(1,128)} %rows_ref.1) | copy-start | bytes 1540

commit v2 on v1

--- a/solution.py
+++ b/solution.py
@@ -65,10 +65,11 @@
 
 
 def body(
-    sizes, cnt_ref, rows_ref, pick_ref, targ_ref, points_hbm, weights_hbm, core_hbm,
-    bg_ref, dir_ref,
+    sizes, cnt_hbm, rows_hbm, pick_hbm, targ_hbm, points_hbm, weights_hbm, core_hbm,
+    slab_ref, rest_ref, fix_ref,
+    cnt_ref, rows_ref, pick_ref, targ_ref,
     pts_v, wts_v, core_v, psq, core_hi, core_lo,
-    xbuf, part, subr, lsum, lrec, skx, kern, pj, pjr, psum, prec, fbuf,
+    xbuf, part, subr, lsum, lrec, skx, out_hi, out_lo, pj, pjr, psum, prec, fbuf,
     in_sem, ag_s, ag_r, fw_s, fw_r, sb_s, sb_r, ln_s, ln_r, sk_s, sk_r,
     pe_s, pe_r, rs_s, rs_r, fa_s, fa_r, ff_s, ff_r,
 ):
@@ -94,12 +95,16 @@
             device_id=dev, device_id_type=MESH,
         )
 
-    in_pts = pltpu.make_async_copy(points_hbm, pts_v, in_sem.at[0])
-    in_wts = pltpu.make_async_copy(weights_hbm, wts_v, in_sem.at[1])
-    in_core = pltpu.make_async_copy(core_hbm, core_v, in_sem.at[2])
-    in_pts.start()
-    in_wts.start()
-    in_core.start()
+    loads = [
+        pltpu.make_async_copy(src, dst, in_sem.at[i])
+        for i, (src, dst) in enumerate((
+            (cnt_hbm, cnt_ref), (rows_hbm, rows_ref), (points_hbm, pts_v), (weights_hbm, wts_v),
+            (pick_hbm, pick_ref), (targ_hbm, targ_ref), (core_hbm, core_v),
+        ))
+    ]
+    for load in loads:
+        load.start()
+    in_cnt, in_rows, in_pts, in_wts, in_pick, in_targ, in_core = loads
 
     barrier = pltpu.get_barrier_semaphore()
     pl.semaphore_signal(barrier, inc=1, device_id=sibling, device_id_type=MESH)
@@ -109,6 +114,8 @@
 
     each(1, n_q, greet)
 
+    in_cnt.wait()
+    in_rows.wait()
     own_count = cnt_ref[0, p * n_s + s]
     used = lax.broadcasted_iota(jnp.int32, (cap, 1), 0) < own_count
     rows = jnp.where(used, column(rows_ref[0].astype(F32)), -1.0)
@@ -146,15 +153,14 @@
         x = xbuf[pk].reshape(n_s * cap, width)
         left = sq_col(x) * c2
 
-        def add(i, acc):
-            at = pl.ds(pl.multiple_of(i * step, step), step)
+        acc = jnp.zeros((n_s * cap, outs), F32)
+        for i in range(n_pts // step):
+            at = slice(i * step, (i + 1) * step)
             inner = mm(x, pts_v[at, :], NT)
             vals = jnp.exp2((inner * (2.0 * c2) - left) - psq[:, at])
             high, low = split2(vals)
             w = wts_v[at, :]
-            return acc + (mm(high, w) + mm(low, w))
-
-        acc = lax.fori_loop(0, n_pts // step, add, jnp.zeros((n_s * cap, outs), F32))
+            acc = acc + (mm(high, w) + mm(low, w))
         part[pk] = acc.reshape(n_s, cap, outs)
         rc(part.at[pk, other], subr.at[pk], sb_s.at[pk], sb_r.at[pk], sibling).start()
 
@@ -199,6 +205,7 @@
         local = slot - o * cap
         rank_of = jnp.where((local >= 0) & (local < have), local + before, rank_of)
         before = before + have
+    in_pick.wait()
     picks = column(pick_ref[...].astype(F32))
     onehot = jnp.where(picks == rank_of.astype(F32), 1.0, 0.0).astype(BF16)
     skx[c] = mm(onehot, xbuf[...].reshape(owners * cap, width)).astype(BF16)
@@ -220,7 +227,10 @@
     sketch = skx[...].reshape(rank, width)
     kern_t = jnp.exp2((mm(sketch, own_x, NT) * (2.0 * c2) - sq_col(sketch) * c2) - sq_row(own_x) * c2)
     kern_t = split2(kern_t)
-    kern[...] = jnp.exp2((mm(own_x, sketch, NT) * (2.0 * c2) - sq_col(own_x) * c2) - sq_row(sketch) * c2)
+    kern = jnp.exp2((mm(own_x, sketch, NT) * (2.0 * c2) - sq_col(own_x) * c2) - sq_row(sketch) * c2)
+    high, low = split2(mm3(split2(kern), (core_hi[...], core_lo[...])))
+    out_hi[...] = high
+    out_lo[...] = low
 
     sub_wait(p)
     slab = part[p, s] + subr[p]
@@ -228,9 +238,13 @@
         pk = mix(p, k, n_p)
         rc(lsum.at[pk], lrec.at[pk], ln_s.at[pk], ln_r.at[pk], {"pts": pk}).wait_recv()
         slab = slab + lrec[pk]
+    in_targ.wait()
     used_f = used.astype(F32)
-    grad = used_f * (slab + RIDGE_COEF * alpha - targ_ref[0].astype(F32))
-    bg_ref[0] = grad
+    rest = used_f * (RIDGE_COEF * alpha - targ_ref[0].astype(F32))
+    slab = used_f * slab
+    slab_ref[0] = slab
+    rest_ref[0] = rest
+    grad = slab + rest
 
     proj = mm3(kern_t, split2(grad))
     if half < n_q * piece:
@@ -277,14 +291,15 @@
         ff(mix(q, k, n_q), s).start()
 
     each(1, n_q, relay)
+
+    def correct(h):
+        block = fbuf[h].reshape(n_q * piece, outs)[0:half, :]
+        cols = pl.ds(pl.multiple_of(h * half, half), half)
+        return mm3((out_hi[:, cols], out_lo[:, cols]), split2(block))
+
+    fix = correct(s)
     each(0, n_q, lambda k: ff(mix(q, k, n_q), other).wait_recv())
-
-    weighted = jnp.zeros((rank, outs), F32)
-    for h in range(n_s):
-        block = fbuf[h].reshape(n_q * piece, outs)[0:half, :]
-        cols = slice(h * half, (h + 1) * half)
-        weighted = weighted + mm3((core_hi[:, cols], core_lo[:, cols]), split2(block))
-    dir_ref[0] = used_f * (grad - mm3(split2(kern[...]), split2(weighted)))
+    fix_ref[0] = used_f * (fix + correct(other))
 
     def lane_done(k):
         pk = mix(p, k, n_p)
@@ -319,16 +334,19 @@
     piece = max(8, -(-rank // (n_s * n_q)))
     sizes = (n_p, n_c, n_s, cap, width, outs, n_pts, n_sk, rank, piece)
     vmem = pl.BlockSpec(memory_space=pltpu.VMEM)
-    smem = pl.BlockSpec(memory_space=pltpu.SMEM)
     hbm = pl.BlockSpec(memory_space=pl.ANY)
     dma = pltpu.SemaphoreType.DMA
     out = jax.ShapeDtypeStruct((1, cap, outs), F32)
-    return pl.pallas_call(
+    slab, rest, fix = pl.pallas_call(
         functools.partial(body, sizes),
-        out_shape=(out, out),
-        in_specs=[smem, vmem, vmem, vmem, hbm, hbm, hbm],
-        out_specs=(vmem, vmem),
+        out_shape=(out, out, out),
+        in_specs=[hbm] * 7,
+        out_specs=(vmem, vmem, vmem),
         scratch_shapes=[
+            pltpu.SMEM(tile_count.shape, jnp.int32),
+            pltpu.VMEM(tile_rows.shape, jnp.int32),
+            pltpu.VMEM(sketch_pick.shape, jnp.int32),
+            pltpu.VMEM(block_targets.shape, BF16),
             pltpu.VMEM((n_pts, width), BF16),
             pltpu.VMEM((n_pts, outs), BF16),
             pltpu.VMEM((rank, rank), F32),
@@ -341,13 +359,14 @@
             pltpu.VMEM((n_p, cap, outs), F32),
             pltpu.VMEM((n_p, cap, outs), F32),
             pltpu.VMEM((n_c, n_sk, width), BF16),
-            pltpu.VMEM((cap, rank), F32),
+            pltpu.VMEM((cap, rank), BF16),
+            pltpu.VMEM((cap, rank), BF16),
             pltpu.VMEM((n_s, n_q * piece, outs), F32),
             pltpu.VMEM((n_q * piece, outs), F32),
             pltpu.VMEM((n_q, piece, outs), F32),
             pltpu.VMEM((n_q, piece, outs), F32),
             pltpu.VMEM((n_s, n_q, piece, outs), F32),
-            dma((3,)),
+            dma((7,)),
             dma((n_p,)), dma((n_p,)),
             dma((n_p,)), dma((n_p,)),
             dma((n_p,)), dma((n_p,)),
@@ -359,9 +378,11 @@
             dma((n_q,)), dma((n_q,)),
         ],
         compiler_params=pltpu.CompilerParams(
-            collective_id=0, has_side_effects=True, vmem_limit_bytes=48 * 1024 * 1024
+            collective_id=0, has_side_effects=True, vmem_limit_bytes=60 * 1024 * 1024
         ),
     )(tile_count, tile_rows, sketch_pick, block_targets, points, weights, core_inv)
+    grad = slab + rest
+    return grad, grad - fix
 
 
 def solution(mesh):

time: 48.6 us -> 40.6 us (0.84)
  local copies, waits for them, and re-layouts: 7.49 us -> 0 us
  Pallas kernels: 40.1 us -> 38.2 us
  other arithmetic: 0 us -> 1.56 us
    unnamed x16 -> x0, local copies, waits for them, and re-layouts: 7.49 us -> none
    pallas_call x1, Pallas kernels: 40.1 us -> 38.2 us  [per_device(): pl.pallas_call(functools.partial(body, sizes), out_shape=(out, out, out),...]
    sub x0 -> x1, other arithmetic: none -> 1.56 us  [per_device(): return (grad, grad - fix)]
where the time goes in v2:
time: 40.6 us; the launch traced here: 40.4 us
  Pallas kernels  38.2 us (94%)
  other arithmetic  1.56 us (4%)
  between operations  0.64 us (2%)
    pallas_call x1, Pallas kernels, per_device(): pl.pallas_call(functools.partial(body, sizes), out_shape=(out, out, out),...  38.2 us
    sub x1, other arithmetic, per_device(): return (grad, grad - fix)  1.56 us

profile of v2, /device:TPU:1, one launch (start us, length us, event | category | flops | bytes accessed | tf_op | source)
XLA Modules:
  0.0 40.4 jit_solution(6875650665310820532)
XLA Ops:
  0.6 38.2 %shard_map.86 = (f32[1,128,128]{2,1,0:T(8,128)}, f32[1,128,128]{2,1,0:T(8,128)}, f32[1,128,128]{2,1,0:T(8,128)}) custom-call(s32[1,8]{1,0:T(1,128)} %cnt_hbm.1, s32[1,1,128]{2,1,0:T(1,128)} %rows_hbm.1, s32[1,256]{1,0:T(1,128)} %pick_hbm.1, bf16[1,128,128]{2,1,0:T(8,128)(2,1)} %targ_hbm.1, bf16[2048,256]{1,0:T(8,128)(2,1)} %points_hbm.1, ...), custom_call_target="tpu_custom_call" | custom-call | tf_op jit(solution)/shard_map/pallas_call | solution.py:340
  38.9 1.6 %fusion = (f32[1,128,128]{2,1,0:T(8,128)}, f32[1,128,128]{2,1,0:T(8,128)}) fusion(f32[1,128,128]{2,1,0:T(8,128)} %get-tuple-element.7, f32[1,128,128]{2,1,0:T(8,128)} %get-tuple-element.5, f32[1,128,128]{2,1,0:T(8,128)} %get-tuple-element.6), kind=kLoop, calls=%fused_computation | loop fusion | flops 32768 | bytes 327680 | tf_op jit(solution)/shard_map/sub | solution.py:385

commit v3 on v2

--- a/solution.py
+++ b/solution.py
@@ -69,7 +69,7 @@
     slab_ref, rest_ref, fix_ref,
     cnt_ref, rows_ref, pick_ref, targ_ref,
     pts_v, wts_v, core_v, psq, core_hi, core_lo,
-    xbuf, part, subr, lsum, lrec, skx, out_hi, out_lo, pj, pjr, psum, prec, fbuf,
+    xbuf, part, subr, lsum, lrec, skx, out_hi, out_lo, gbuf, psum, prec, fbuf,
     in_sem, ag_s, ag_r, fw_s, fw_r, sb_s, sb_r, ln_s, ln_r, sk_s, sk_r,
     pe_s, pe_r, rs_s, rs_r, fa_s, fa_r, ff_s, ff_r,
 ):
@@ -109,10 +109,11 @@
     barrier = pltpu.get_barrier_semaphore()
     pl.semaphore_signal(barrier, inc=1, device_id=sibling, device_id_type=MESH)
 
-    def greet(k):
-        pl.semaphore_signal(barrier, inc=1, device_id=at_q(k)[1], device_id_type=MESH)
-
-    each(1, n_q, greet)
+    def greet(dev):
+        pl.semaphore_signal(barrier, inc=1, device_id=dev, device_id_type=MESH)
+
+    each(1, n_p, lambda k: greet({"pts": mix(p, k, n_p)}))
+    each(1, n_c, lambda k: greet({"col": mix(c, k, n_c)}))
 
     in_cnt.wait()
     in_rows.wait()
@@ -123,7 +124,7 @@
     pick_rows = jnp.where(rows == ids, 1.0, 0.0).astype(BF16)
     in_pts.wait()
     xbuf[p, s] = mm(pick_rows, pts_v[...]).astype(BF16)
-    pl.semaphore_wait(barrier, n_q)
+    pl.semaphore_wait(barrier, n_p + n_c - 1)
 
     def fw(pk, slot):
         return rc(xbuf.at[pk, slot], xbuf.at[pk, slot], fw_s.at[pk], fw_r.at[pk], sibling)
@@ -208,10 +209,14 @@
     in_pick.wait()
     picks = column(pick_ref[...].astype(F32))
     onehot = jnp.where(picks == rank_of.astype(F32), 1.0, 0.0).astype(BF16)
-    skx[c] = mm(onehot, xbuf[...].reshape(owners * cap, width)).astype(BF16)
+    def rows_of(k):
+        return pl.ds(pl.multiple_of(k * n_sk, n_sk), n_sk)
+
+    skx[rows_of(c), :] = mm(onehot, xbuf[...].reshape(owners * cap, width)).astype(BF16)
 
     def sk(ck, mine):
-        return rc(skx.at[mine], skx.at[mine], sk_s.at[ck], sk_r.at[mine], {"col": ck})
+        at = skx.at[rows_of(mine), :]
+        return rc(at, at, sk_s.at[ck], sk_r.at[mine], {"col": ck})
 
     each(1, n_c, lambda k: sk(mix(c, k, n_c), c).start())
     if n_p > 1:
@@ -224,8 +229,10 @@
 
     each(1, n_c, lambda k: sk(mix(c, k, n_c), mix(c, k, n_c)).wait_recv())
     own_x = xbuf[p, s]
-    sketch = skx[...].reshape(rank, width)
-    kern_t = jnp.exp2((mm(sketch, own_x, NT) * (2.0 * c2) - sq_col(sketch) * c2) - sq_row(own_x) * c2)
+    sketch = skx[...]
+    pair_x = xbuf[p].reshape(n_s * cap, width)
+    mine_x = skx[pl.ds(pl.multiple_of(s * half, half), half), :]
+    kern_t = jnp.exp2((mm(mine_x, pair_x, NT) * (2.0 * c2) - sq_col(mine_x) * c2) - sq_row(pair_x) * c2)
     kern_t = split2(kern_t)
     kern = jnp.exp2((mm(own_x, sketch, NT) * (2.0 * c2) - sq_col(own_x) * c2) - sq_row(sketch) * c2)
     high, low = split2(mm3(split2(kern), (core_hi[...], core_lo[...])))
@@ -246,15 +253,14 @@
     rest_ref[0] = rest
     grad = slab + rest
 
-    proj = mm3(kern_t, split2(grad))
+    gbuf[s] = grad
+    pe = rc(gbuf.at[s], gbuf.at[s], pe_s, pe_r, sibling)
+    pe.start()
+    rc(gbuf.at[other], gbuf.at[other], pe_s, pe_r, sibling).wait_recv()
+    proj = mm3(kern_t, split2(gbuf[...].reshape(n_s * cap, outs)))
     if half < n_q * piece:
-        pj[...] = jnp.zeros_like(pj)
-    for h in range(n_s):
-        pj[h, 0:half, :] = proj[h * half:(h + 1) * half, :]
-    pe = rc(pj.at[other], pjr, pe_s, pe_r, sibling)
-    pe.start()
-    pe.wait_recv()
-    psum[...] = (pj[s] + pjr[...]).reshape(n_q, piece, outs)
+        proj = jnp.concatenate([proj, jnp.zeros((n_q * piece - half, outs), F32)], axis=0)
+    psum[...] = proj.reshape(n_q, piece, outs)
 
     def rs(k, mine):
         peer, dev = at_q(k)
@@ -358,11 +364,10 @@
             pltpu.VMEM((n_p, cap, outs), F32),
             pltpu.VMEM((n_p, cap, outs), F32),
             pltpu.VMEM((n_p, cap, outs), F32),
-            pltpu.VMEM((n_c, n_sk, width), BF16),
+            pltpu.VMEM((n_c * n_sk, width), BF16),
             pltpu.VMEM((cap, rank), BF16),
             pltpu.VMEM((cap, rank), BF16),
-            pltpu.VMEM((n_s, n_q * piece, outs), F32),
-            pltpu.VMEM((n_q * piece, outs), F32),
+            pltpu.VMEM((n_s, cap, outs), F32),
             pltpu.VMEM((n_q, piece, outs), F32),
             pltpu.VMEM((n_q, piece, outs), F32),
             pltpu.VMEM((n_s, n_q, piece, outs), F32),

time: 40.6 us -> 39.4 us (0.970)
  Pallas kernels: 38.2 us -> 37 us
    pallas_call x1, Pallas kernels: 38.2 us -> 37 us  [per_device(): pl.pallas_call(functools.partial(body, sizes), out_shape=(out, out, out),...]
where the time goes in v3:
time: 39.4 us; the launch traced here: 39.2 us
  Pallas kernels  37 us (94%)
  other arithmetic  1.56 us (4%)
  between operations  0.64 us (2%)
    pallas_call x1, Pallas kernels, per_device(): pl.pallas_call(functools.partial(body, sizes), out_shape=(out, out, out),...  37 us
    sub x1, other arithmetic, per_device(): return (grad, grad - fix)  1.56 us

profile of v3, /device:TPU:1, one launch (start us, length us, event | category | flops | bytes accessed | tf_op | source)
XLA Modules:
  0.0 39.2 jit_solution(15877297811450797162)
XLA Ops:
  0.6 37.0 %shard_map.86 = (f32[1,128,128]{2,1,0:T(8,128)}, f32[1,128,128]{2,1,0:T(8,128)}, f32[1,128,128]{2,1,0:T(8,128)}) custom-call(s32[1,8]{1,0:T(1,128)} %cnt_hbm.1, s32[1,1,128]{2,1,0:T(1,128)} %rows_hbm.1, s32[1,256]{1,0:T(1,128)} %pick_hbm.1, bf16[1,128,128]{2,1,0:T(8,128)(2,1)} %targ_hbm.1, bf16[2048,256]{1,0:T(8,128)(2,1)} %points_hbm.1, ...), custom_call_target="tpu_custom_call" | custom-call | tf_op jit(solution)/shard_map/pallas_call | solution.py:346
  37.7 1.6 %fusion = (f32[1,128,128]{2,1,0:T(8,128)}, f32[1,128,128]{2,1,0:T(8,128)}) fusion(f32[1,128,128]{2,1,0:T(8,128)} %get-tuple-element.7, f32[1,128,128]{2,1,0:T(8,128)} %get-tuple-element.5, f32[1,128,128]{2,1,0:T(8,128)} %get-tuple-element.6), kind=kLoop, calls=%fused_computation | loop fusion | flops 32768 | bytes 327680 | tf_op jit(solution)/shard_map/sub | solution.py:390
